TPU v7x, 128 devices: a whole 4x4x4 slice. The times are simulated.
128 devices in a mesh: rep: 4 (over y_lo, core), fsdp: 32 (over x, y_hi, z).
Axes of the slice: x: 4, y: 4 (y_hi: 2, y_lo: 2; y = y_hi * 2 + y_lo), z: 4, core: 2. Of those that a mesh axis runs over, the one named last changes fastest.
Arguments:
- features: bfloat16 [4, 12288, 896], P('rep', 'fsdp'), may hold values from -6 to 6
- cotangent: bfloat16 [4, 12288, 4864], P('rep', 'fsdp'), may hold values from -6 to 6
- gate_weight: bfloat16 [4, 4864, 896], P('rep', 'fsdp'), may hold values from -6 to 6
- up_weight: bfloat16 [4, 4864, 896], P('rep', 'fsdp'), may hold values from -6 to 6
- gate_moment: bfloat16 [4, 4864, 896], P('rep', 'fsdp'), may hold values from -6 to 6
- up_moment: bfloat16 [4, 4864, 896], P('rep', 'fsdp'), may hold values from -6 to 6
- step_index: int32 [], replicated, may hold values from 0 to 999
Outputs:
- new_gate: bfloat16 [4, 4864, 896], P('rep', 'fsdp')
- new_up: bfloat16 [4, 4864, 896], P('rep', 'fsdp')
- new_gate_moment: bfloat16 [4, 4864, 896], P('rep', 'fsdp')
- new_up_moment: bfloat16 [4, 4864, 896], P('rep', 'fsdp')
All inputs are finite; a program needn't handle non-finite values.
Results may differ from a plain program's by a relative error of at most 0.03.
Values may be sent and summed in bfloat16 or wider, within the bound.
A program may use at most 128 MiB of HBM per device.

v0:
```python
import jax
import jax.numpy as jnp
from jax import lax
from jax.sharding import PartitionSpec as P

moment_decay = 0.9
step_rate = 0.5


def shortened(value):

    def short(part):
        return part.astype(jnp.bfloat16) if part.dtype == jnp.float32 else part

    return jax.tree.map(short, value)


def swapped(value, axis, stride):
    mask = 2**stride
    pairs = [(source, source ^ mask) for source in range(lax.axis_size(axis))]
    return lax.ppermute(value, axis, pairs)


def derivatives(gate, upward, tangent, factor):
    sigma = jax.nn.sigmoid(gate)
    gate_diff = (factor * tangent * upward * sigma * (1.0 + gate * (1.0 - sigma))).astype(
        jnp.bfloat16
    )
    upward_diff = (factor * tangent * gate * sigma).astype(jnp.bfloat16)
    return (gate_diff, upward_diff)


def project(left, right):
    return lax.dot_general(
        left, right, (((1,), (1,)), ((), ())), preferred_element_type=jnp.float32
    )


def swapper(which_bit):

    def run_swap(paired):
        return jax.tree.map(
            lambda part, own: part.astype(own.dtype),
            swapped(shortened(paired), "rep", which_bit),
            paired,
        )

    return run_swap


def body(features, cotangent, gate_weight, up_weight, gate_moment, up_moment, step_index):
    local_feat = features[0]
    local_tangent = cotangent[0]
    local_gate = gate_weight[0]
    local_up = up_weight[0]
    width = local_feat.shape[1]
    factor = width ** (-0.5)
    part_gate = project(local_feat, lax.all_gather(local_gate, "fsdp", axis=0, tiled=True)) * factor
    part_up = project(local_feat, lax.all_gather(local_up, "fsdp", axis=0, tiled=True)) * factor
    gate_diff, upward_diff = derivatives(
        part_gate, part_up, local_tangent.astype(jnp.float32), factor
    )
    term_gate = lax.dot_general(
        gate_diff, local_feat, (((0,), (0,)), ((), ())), preferred_element_type=jnp.float32
    )
    term_up = lax.dot_general(
        upward_diff, local_feat, (((0,), (0,)), ((), ())), preferred_element_type=jnp.float32
    )
    summed = lax.psum_scatter(
        jnp.stack([term_gate, term_up], axis=1).astype(jnp.bfloat16),
        "fsdp",
        scatter_dimension=0,
        tiled=True,
    ).astype(jnp.float32)
    grad_gate = summed[:, 0]
    grad_up = summed[:, 1]
    moment_gate = (moment_decay * gate_moment[0].astype(jnp.float32) + grad_gate).astype(
        jnp.bfloat16
    )
    moment_up = (moment_decay * up_moment[0].astype(jnp.float32) + grad_up).astype(jnp.bfloat16)
    stepped_gate = (
        local_gate.astype(jnp.float32) - step_rate * moment_gate.astype(jnp.float32)
    ).astype(jnp.bfloat16)
    stepped_up = (local_up.astype(jnp.float32) - step_rate * moment_up.astype(jnp.float32)).astype(
        jnp.bfloat16
    )
    paired = jnp.stack([stepped_gate, stepped_up])
    nbits = lax.axis_size("rep").bit_length() - 1
    branches = [swapper(which_bit) for which_bit in range(nbits)]
    other = lax.switch(step_index % nbits, branches, paired)
    averaged = ((paired.astype(jnp.float32) + other.astype(jnp.float32)) * 0.5).astype(jnp.bfloat16)
    return (averaged[0][None], averaged[1][None], moment_gate[None], moment_up[None])


def solution(mesh):
    in_specs = (
        P("rep", "fsdp", None),
        P("rep", "fsdp", None),
        P("rep", "fsdp", None),
        P("rep", "fsdp", None),
        P("rep", "fsdp", None),
        P("rep", "fsdp", None),
        P(),
    )
    out_specs = (
        P("rep", "fsdp", None),
        P("rep", "fsdp", None),
        P("rep", "fsdp", None),
        P("rep", "fsdp", None),
    )
    return jax.shard_map(body, mesh=mesh, in_specs=in_specs, out_specs=out_specs, check_vma=False)
```

profile of v0, /device:TPU:0, one launch (start us, length us, event | category | flops | bytes accessed | tf_op | source)
XLA Modules:
  0.0 495.2 jit_solution(8066677821737097570)
XLA Ops:
  7.2 0.0 copy-start
  7.2 0.0 all-gather.7.cloned.1.call-start
  7.2 0.7 all-gather.7.cloned.1.call-update
  7.9 0.0 all-gather.5.cloned.1.call-start
  8.0 0.7 all-gather.5.cloned.1.call-update
  8.7 0.0 reduce-scatter.4.cloned.1.call-start
  8.7 110.7 %all-gather.7.cloned.1.call-done = bf16[1,4864,896]{2,1,0:T(8,128)(2,1)} async-done(((bf16[1,152,896]{2,1,0:T(8,128)(2,1)}), bf16[1,4864,896]{2,1,0:T(8,128)(2,1)}) %all-gather.7.cloned.1.call-update) | async-done | bytes 8716304 | tf_op jit(solution)/shard_map/all_gather | solution.py:58
  119.4 0.0 copy-done
  119.4 0.0 copy-start.6
  119.4 6.8 %fusion.13 = f32[384,4864]{1,0:T(8,128)S(1)} fusion(bf16[1,4864,896]{2,1,0:T(8,128)(2,1)} %all-gather.7.cloned.1.call-done, bf16[1,384,896]{2,1,0:T(8,128)(2,1)S(1)} %copy-done), kind=kOutput, calls=%fused_computation.18 | convolution fusion | flops 3348922368 | bytes 16875520 | tf_op jit(solution)/shard_map/dot_general | solution.py:34
  126.3 0.0 copy-start.7
  126.3 3.0 copy-done.7
  129.2 0.0 copy-done.6
  129.2 7.8 %fusion.5 = bf16[4864,1,896]{2,0,1:T(8,128)(2,1)} fusion(f32[384,4864]{1,0:T(8,128)S(1)} %fusion.13, bf16[1,384,4864]{2,1,0:T(8,128)(2,1)S(1)} %copy-done.6, bf16[1,384,896]{2,1,0:T(8,128)(2,1)S(1)} %copy-done), kind=kOutput, calls=%fused_computation.8 | convolution fusion | flops 3366354944 | bytes 20611072 | tf_op jit(solution)/shard_map/dot_general | solution.py:66
  137.0 89.1 %all-gather.5.cloned.1.call-done = bf16[1,4864,896]{2,1,0:T(8,128)(2,1)} async-done(((bf16[1,152,896]{2,1,0:T(8,128)(2,1)}), bf16[1,4864,896]{2,1,0:T(8,128)(2,1)}) %all-gather.5.cloned.1.call-update) | async-done | bytes 8716304 | tf_op jit(solution)/shard_map/all_gather | solution.py:59
  226.1 15.7 %fusion.4 = bf16[4864,1,896]{2,0,1:T(8,128)(2,1)} fusion(bf16[1,384,896]{2,1,0:T(8,128)(2,1)S(1)} %copy-done, f32[384,4864]{1,0:T(8,128)} %copy-done.7, bf16[1,384,4864]{2,1,0:T(8,128)(2,1)} %param.10, bf16[1,4864,896]{2,1,0:T(8,128)(2,1)} %all-gather.5.cloned.1.call-done), kind=kOutput, calls=%fused_computation.7 | convolution fusion | flops 6722748416 | bytes 29327360 | tf_op jit(solution)/shard_map/dot_general | solution.py:63
  241.8 8.3 %maximum_bitcast_fusion = bf16[2,608,8,896]{3,2,1,0:T(8,128)(2,1)S(1)} fusion(bf16[4864,1,896]{2,0,1:T(8,128)(2,1)} %fusion.5, bf16[4864,1,896]{2,0,1:T(8,128)(2,1)} %fusion.4), kind=kLoop, calls=%fused_computation | loop fusion | flops 8716288 | bytes 34865152
  250.1 6.9 %copy.14 = bf16[2,608,8,896]{3,2,0,1:T(8,128)(2,1)} copy(bf16[2,608,8,896]{3,2,1,0:T(8,128)(2,1)S(1)} %maximum_bitcast_fusion) | data formatting | bytes 34865152
  257.0 0.0 copy-start.2
  257.0 0.0 copy-start.3
  257.0 0.0 copy-start.4
  257.0 0.0 copy-start.5
  257.0 0.0 reduce-scatter.4.cloned.1.call-update
  257.0 0.0 copy-start.1
  257.8 224.3 %reduce-scatter.4.cloned.1.call-done = bf16[152,1792]{1,0:T(8,128)(2,1)} async-done(((bf16[4864,1792]{1,0:T(8,128)(2,1)}), bf16[152,1792]{1,0:T(8,128)(2,1)}) %reduce-scatter.4.cloned.1.call-update) | async-done | bytes 544784
  482.2 1.1 bitcast_convert_fusion
  483.3 0.0 copy-done.2
  483.3 0.0 copy-done.3
  483.3 0.0 copy-done.4
  483.3 0.0 copy-done.5
  483.3 1.1 subtract_convert_fusion.1
  484.4 0.1 pad_maximum_fusion
  484.5 2.2 conditional.4
  484.5 0.1 collective-permute-start
  484.6 2.1 collective-permute-done
  486.7 1.2 multiply_convert_fusion
  487.9 0.8 fusion.35
  488.7 0.0 copy-done.1
Async XLA Ops:
  7.2 112.3 %copy-start = (bf16[1,384,896]{2,1,0:T(8,128)(2,1)S(1)}, bf16[1,384,896]{2,1,0:T(8,128)(2,1)}, u32[]{:S(2)}) copy-start(bf16[1,384,896]{2,1,0:T(8,128)(2,1)} %param.9) | copy-start | bytes 2064388
  7.2 112.3 %all-gather.7.cloned.1.call-start = ((), (), s32[]{:S(2)}) async-start(), calls=%async_computation.2 | async-start | bytes 8988672 | tf_op jit(solution)/shard_map/all_gather | solution.py:58
  7.9 218.2 %all-gather.5.cloned.1.call-start = ((), (), s32[]{:S(2)}) async-start(), calls=%async_computation.1 | async-start | bytes 8988672 | tf_op jit(solution)/shard_map/all_gather | solution.py:59
  8.7 473.5 %reduce-scatter.4.cloned.1.call-start = ((), (), s32[]{:S(2)}) async-start(), calls=%async_computation.3 | async-start | bytes 17977344
  119.4 9.8 %copy-start.6 = (bf16[1,384,4864]{2,1,0:T(8,128)(2,1)S(1)}, bf16[1,384,4864]{2,1,0:T(8,128)(2,1)}, u32[]{:S(2)}) copy-start(bf16[1,384,4864]{2,1,0:T(8,128)(2,1)} %param.10) | copy-start | bytes 11206660
  126.3 3.0 copy-start.7
  257.0 226.3 %copy-start.2 = (bf16[1,152,896]{2,1,0:T(8,128)(2,1)S(1)}, bf16[1,152,896]{2,1,0:T(8,128)(2,1)}, u32[]{:S(2)}) copy-start(bf16[1,152,896]{2,1,0:T(8,128)(2,1)} %param.11) | copy-start | bytes 817156
  257.0 226.3 %copy-start.3 = (bf16[1,152,896]{2,1,0:T(8,128)(2,1)S(1)}, bf16[1,152,896]{2,1,0:T(8,128)(2,1)}, u32[]{:S(2)}) copy-start(bf16[1,152,896]{2,1,0:T(8,128)(2,1)} %param.12) | copy-start | bytes 817156
  257.0 226.3 %copy-start.4 = (bf16[1,152,896]{2,1,0:T(8,128)(2,1)S(1)}, bf16[1,152,896]{2,1,0:T(8,128)(2,1)}, u32[]{:S(2)}) copy-start(bf16[1,152,896]{2,1,0:T(8,128)(2,1)} %param.13) | copy-start | bytes 817156
  257.0 226.3 %copy-start.5 = (bf16[1,152,896]{2,1,0:T(8,128)(2,1)S(1)}, bf16[1,152,896]{2,1,0:T(8,128)(2,1)}, u32[]{:S(2)}) copy-start(bf16[1,152,896]{2,1,0:T(8,128)(2,1)} %param.14) | copy-start | bytes 817156
  257.0 231.7 %copy-start.1 = (bf16[1,384,896]{2,1,0:T(8,128)(2,1)S(1)}, bf16[1,384,896]{2,1,0:T(8,128)(2,1)}, u32[]{:S(2)}) copy-start(bf16[1,384,896]{2,1,0:T(8,128)(2,1)} %param.9) | copy-start | bytes 2064388
  484.5 2.2 collective-permute-start
Sparse Core Ops, SparseCore 0:
  11.0 108.4 all-gather.6
  122.4 103.6 all-gather.4
  257.2 224.9 reduce-scatter.3
where the time goes:
time: 497 us; the launch traced here: 495 us
  waiting for transfers between devices  428 us (86%)
  matrix products  30.3 us (6%)
  between operations  14.6 us (3%)
  other arithmetic  11.7 us (2%)
  local copies, waits for them, and re-layouts  10.7 us (2%)
    unnamed x4, waiting for transfers between devices  226 us
    all_gather x1, waiting for transfers between devices, body(): lax.all_gather(local_gate, 'fsdp', axis=0, tiled=True)  111 us
    all_gather x1, waiting for transfers between devices, body(): lax.all_gather(local_up, 'fsdp', axis=0, tiled=True)  89.1 us
    dot_general x1, matrix products, body(): lax.dot_general(gate_diff, local_feat, (((0,), (0,)), ((), ())), preferre...  15.7 us
  transfers between devices with their start and end apart: 4, of which 4 were waited for; matrix products, arithmetic and copies ran while one was open for 3% of the time, Pallas kernels for 0%

commit v1 on v0

v1 whole, which is shorter than its diff:
```python
import functools

import jax
import jax.numpy as jnp
from jax import lax
from jax.experimental import pallas as pl
from jax.experimental.pallas import tpu as pltpu
from jax.sharding import PartitionSpec as P

MESH = pl.DeviceIdType.MESH
F32 = jnp.float32
BF16 = jnp.bfloat16
MOMENT_DECAY = 0.9
STEP_RATE = 0.5

NX, NY, NZ = 4, 2, 4
ORDER = ((2, 0), (2, 1), (1, 1), (3, 1), (1, 0), (3, 0), (0, 1), (0, 0))
SLOT = {place: index for index, place in enumerate(ORDER)}
SLOTS = len(ORDER)
AHEAD = 2


def step_kernel(
    stride,
    feat_hbm,
    cot_hbm,
    gate_hbm,
    up_hbm,
    gmom_hbm,
    umom_hbm,
    new_gate,
    new_up,
    mom_gate,
    mom_up,
    feat,
    raw,
    turned,
    cots,
    weights,
    moments,
    grad,
    terms,
    relay,
    sums,
    crossed,
    stepped,
    other,
    local_sem,
    feat_send,
    feat_recv,
    w_send,
    w_recv,
    w_fwd,
    cot_send,
    cot_recv,
    term_send,
    relay_recv,
    sum_recv,
    cross_send,
    cross_recv,
    swap_send,
    swap_recv,
):
    tok, width = feat_hbm.shape
    rows = gate_hbm.shape[0]
    half = tok // 2
    factor = width ** (-0.5)
    rep, place = lax.axis_index("rep"), lax.axis_index("fsdp")
    x, y, z = place // (NY * NZ), lax.rem(place // NZ, NY), lax.rem(place, NZ)

    def at(dx, dy, dz):
        return (
            rep,
            lax.rem(x + dx, NX) * (NY * NZ) + lax.rem(y + dy, NY) * NZ + lax.rem(z + dz, NZ),
        )

    if stride == 1:
        mate = (rep + 1 - 2 * lax.rem(rep, 2), place)
    else:
        mate = (lax.rem(rep + 2, 4), place)
    across = at(0, 1, 0)
    along_x = {dx: at(dx, 0, 0) for dx in (1, 2, 3)}
    along_z = {dz: at(0, 0, dz) for dz in (1, 3)}

    def copy(src, dst, send, recv, target):
        return pltpu.make_async_remote_copy(
            src_ref=src, dst_ref=dst, send_sem=send, recv_sem=recv, device_id=target, device_id_type=MESH
        )

    barrier = pltpu.get_barrier_semaphore()
    greeted = [mate, across, *along_x.values(), *along_z.values()]
    for target in greeted:
        pl.semaphore_signal(barrier, inc=1, device_id=target, device_id_type=MESH)
    pl.semaphore_wait(barrier, len(greeted))

    own = SLOT[0, 0]
    local = [
        pltpu.make_async_copy(cot_hbm, raw, local_sem.at[0]),
        pltpu.make_async_copy(feat_hbm, feat.at[pl.ds(0, tok)], local_sem.at[1]),
        pltpu.make_async_copy(gate_hbm, weights.at[own, 0], local_sem.at[2]),
        pltpu.make_async_copy(up_hbm, weights.at[own, 1], local_sem.at[3]),
        pltpu.make_async_copy(gmom_hbm, moments.at[0], local_sem.at[4]),
        pltpu.make_async_copy(umom_hbm, moments.at[1], local_sem.at[5]),
    ]
    for item in local:
        item.start()

    mine = (gate_hbm, up_hbm)
    partner = SLOT[0, 1]

    def w_cross(kind):
        return copy(mine[kind], weights.at[partner, kind], w_send.at[0, kind], w_recv.at[partner, kind], across)

    def w_next(dz, dy, kind):
        source = mine[kind] if dy == 0 else weights.at[partner, kind]
        slot = SLOT[NZ - dz, dy]
        return copy(
            source, weights.at[slot, kind], w_send.at[1 + dz // 2 + 2 * dy, kind], w_recv.at[slot, kind], along_z[dz]
        )

    def w_on(dz, dy):
        kind = 0 if dz == 1 else 1
        slot = SLOT[2, dy]
        return copy(
            weights.at[SLOT[NZ - dz, dy], kind], weights.at[slot, kind], w_fwd.at[dy, kind], w_recv.at[slot, kind],
            along_z[dz],
        )

    def f_next(dx, part):
        there = feat.at[pl.ds((NX - dx) * tok + part * half, half)]
        source = feat_hbm.at[pl.ds(part * half, half)]
        return copy(source, there, feat_send.at[dx // 2, part], feat_recv.at[dx // 2, part], along_x[dx])

    def f_on(dx):
        part = 0 if dx == 1 else 1
        source = feat.at[pl.ds((NX - dx) * tok + part * half, half)]
        there = feat.at[pl.ds(2 * tok + part * half, half)]
        return copy(source, there, feat_send.at[2, part], feat_recv.at[2, part], along_x[dx])

    def slot_of(index, x_there):
        dz = jnp.where(index < 2, 2, jnp.where(index < 6, jnp.where(lax.rem(index, 2) == 0, 1, 3), 0))
        dy = jnp.where((index == 0) | (index == 4) | (index == 5) | (index == 7), 0, 1)
        return lax.rem(x_there, NX) * (NY * NZ) + lax.rem(y + dy, NY) * NZ + lax.rem(z + dz, NZ)

    def c_send(index, dx):
        source = turned.at[slot_of(index, x + dx)]
        there = NX - dx - 1
        return copy(
            source, cots.at[there, index], cot_send.at[there, index], cot_recv.at[there, index], along_x[dx]
        )

    for kind in (0, 1):
        w_cross(kind).start()
    for kind in (0, 1):
        w_next(1, 0, kind).start()
        w_next(3, 0, 1 - kind).start()
        f_next(1, kind).start()
        f_next(3, 1 - kind).start()

    local[0].wait()
    group = 16 * rows

    def turn(g, carry):
        part = raw[:, pl.ds(pl.multiple_of(g * group, 128), group)].astype(F32).T
        for s in range(16):
            turned[g * 16 + s] = part[s * rows : (s + 1) * rows].astype(BF16)
        return carry

    lax.fori_loop(0, raw.shape[1] // group, turn, 0)

    for dz in (1, 3):
        kind = 0 if dz == 1 else 1
        w_next(dz, 0, kind).wait_recv()
        w_on(dz, 0).start()
    for dx in (1, 3):
        f_next(dx, 0 if dx == 1 else 1).wait_recv()
        f_on(dx).start()
    for kind in (0, 1):
        w_cross(kind).wait_recv()
        for dz in (1, 3):
            w_next(dz, 1, kind).start()
    for index in range(AHEAD):
        for dx in (1, 3, 2):
            c_send(index, dx).start()
    for dz in (1, 3):
        kind = 0 if dz == 1 else 1
        w_next(dz, 1, kind).wait_recv()
        w_on(dz, 1).start()
    for item in local[1:]:
        item.wait()
    f_next(1, 1).wait_recv()
    f_next(3, 0).wait_recv()
    f_on(1).wait_recv()
    f_on(3).wait_recv()

    def t_send(slot, kind):
        dz, dy = ORDER[slot]
        way = {(2, 0): 1, (2, 1): 3}.get((dz, kind), dz)
        if dz == 2:
            there, recv = relay.at[dy, kind], relay_recv.at[dy, kind]
        else:
            side = 0 if dz == 1 else 1
            there, recv = sums.at[side, dy, kind], sum_recv.at[side, dy, kind]
        return copy(terms.at[slot, kind], there, term_send.at[slot, kind], recv, along_z[way])

    def cross(kind):
        return copy(terms.at[partner, kind], crossed.at[kind], cross_send.at[kind], cross_recv.at[kind], across)

    def total(dy, kind):
        for side in (0, 1):
            t_send(SLOT[1 if side == 0 else 3, dy], kind).wait_recv()
        own_term = grad[pl.ds(kind * rows, rows)]
        return own_term + sums[0, dy, kind].astype(F32) + sums[1, dy, kind].astype(F32)

    def chunk(index, carry):
        for slot, (dz, dy) in enumerate(ORDER):
            if dz == 2:
                arrivals = [w_on(1, dy), w_on(3, dy)]
            elif dz == 1:
                arrivals = [w_next(3, dy, 0)]
            elif dz == 3:
                arrivals = [w_next(1, dy, 1)]
            else:
                arrivals = []
            if arrivals:

                @pl.when(index == slot)
                def _():
                    for item in arrivals:
                        item.wait_recv()

        for dx in (1, 3, 2):
            c_send(index, dx).wait_recv()

        @pl.when(index + AHEAD < SLOTS)
        def _():
            for dx in (1, 3, 2):
                c_send(index + AHEAD, dx).start()

        both = jnp.concatenate([weights[index, 0].astype(F32), weights[index, 1].astype(F32)], 0).astype(BF16)
        made = lax.dot_general(both, feat[...], (((1,), (1,)), ((), ())), preferred_element_type=F32) * factor
        gate, upward = made[:rows], made[rows:]
        tangent = jnp.concatenate(
            [turned[slot_of(index, x)].astype(F32)] + [cots[dx, index].astype(F32) for dx in range(NX - 1)], 1
        )
        sigma = jax.nn.sigmoid(gate)
        scaled = factor * tangent * sigma
        gate_diff = scaled * upward * (1.0 + gate * (1.0 - sigma))
        upward_diff = scaled * gate
        diffs = jnp.concatenate([gate_diff, upward_diff], 0).astype(BF16)
        grad[...] = jnp.dot(diffs, feat[...], preferred_element_type=F32)

        for slot, (dz, dy) in enumerate(ORDER[:-1]):

            @pl.when(index == slot)
            def _():
                for kind in (0, 1):
                    if dz == 0:
                        terms[slot, kind] = total(dy, kind).astype(BF16)
                        cross(kind).start()
                    else:
                        term = grad[pl.ds(kind * rows, rows)]
                        if (dz, kind) in ((1, 0), (3, 1)):
                            t_send(SLOT[2, dy], kind).wait_recv()
                            term = term + relay[dy, kind].astype(F32)
                        terms[slot, kind] = term.astype(BF16)
                        t_send(slot, kind).start()

        return carry

    lax.fori_loop(0, SLOTS, chunk, 0)

    def swap(kind):
        return copy(stepped.at[kind], other.at[kind], swap_send.at[kind], swap_recv.at[kind], mate)

    for kind, out in ((0, mom_gate), (1, mom_up)):
        value = total(0, kind)
        cross(kind).wait_recv()
        value = value + crossed[kind].astype(F32)
        moment = (MOMENT_DECAY * moments[kind].astype(F32) + value).astype(BF16)
        out[...] = moment
        stepped[kind] = (weights[own, kind].astype(F32) - STEP_RATE * moment.astype(F32)).astype(BF16)
        swap(kind).start()
    for kind, out in ((0, new_gate), (1, new_up)):
        swap(kind).wait_recv()
        out[...] = ((stepped[kind].astype(F32) + other[kind].astype(F32)) * 0.5).astype(BF16)

    for kind in (0, 1):
        w_cross(kind).wait_send()
        cross(kind).wait_send()
        swap(kind).wait_send()
        for dz in (1, 3):
            for dy in (0, 1):
                w_next(dz, dy, kind).wait_send()
        for dx in (1, 3):
            f_next(dx, kind).wait_send()
        for slot, (dz, dy) in enumerate(ORDER):
            if dz:
                t_send(slot, kind).wait_send()
    for dz in (1, 3):
        for dy in (0, 1):
            w_on(dz, dy).wait_send()
    for dx in (1, 3):
        f_on(dx).wait_send()

    def drain(index, carry):
        for dx in (1, 3, 2):
            c_send(index, dx).wait_send()
        return carry

    lax.fori_loop(0, SLOTS, drain, 0)


def step_call(stride, features, cotangent, gate_weight, up_weight, gate_moment, up_moment):
    tok, width = features.shape
    rows = gate_weight.shape[0]
    hidden = cotangent.shape[1]
    dma = pltpu.SemaphoreType.DMA
    out = jax.ShapeDtypeStruct((rows, width), BF16)
    return pl.pallas_call(
        functools.partial(step_kernel, stride),
        out_shape=(out,) * 4,
        in_specs=[pl.BlockSpec(memory_space=pl.ANY)] * 6,
        out_specs=(pl.BlockSpec(memory_space=pltpu.VMEM),) * 4,
        scratch_shapes=[
            pltpu.VMEM((NX * tok, width), BF16),
            pltpu.VMEM((tok, hidden), BF16),
            pltpu.VMEM((hidden // rows, rows, tok), BF16),
            pltpu.VMEM((NX - 1, SLOTS, rows, tok), BF16),
            pltpu.VMEM((SLOTS, 2, rows, width), BF16),
            pltpu.VMEM((2, rows, width), BF16),
            pltpu.VMEM((2 * rows, width), F32),
            pltpu.VMEM((SLOTS - 1, 2, rows, width), BF16),
            pltpu.VMEM((2, 2, rows, width), BF16),
            pltpu.VMEM((2, 2, 2, rows, width), BF16),
            pltpu.VMEM((2, rows, width), BF16),
            pltpu.VMEM((2, rows, width), BF16),
            pltpu.VMEM((2, rows, width), BF16),
            dma((6,)),
            dma((3, 2)),
            dma((3, 2)),
            dma((5, 2)),
            dma((SLOTS, 2)),
            dma((2, 2)),
            dma((NX - 1, SLOTS)),
            dma((NX - 1, SLOTS)),
            dma((SLOTS - 1, 2)),
            dma((2, 2)),
            dma((2, 2, 2)),
            dma((2,)),
            dma((2,)),
            dma((2,)),
            dma((2,)),
        ],
        compiler_params=pltpu.CompilerParams(
            collective_id=stride - 1, has_side_effects=True, vmem_limit_bytes=56 * 2**20
        ),
        cost_estimate=pl.CostEstimate(
            flops=8 * tok * hidden * width, bytes_accessed=2 * tok * (hidden + width), transcendentals=tok * hidden
        ),
        name=f"step_stride_{stride}",
    )(features, cotangent, gate_weight, up_weight, gate_moment, up_moment)


def body(features, cotangent, gate_weight, up_weight, gate_moment, up_moment, step_index):
    arrays = [a[0] for a in (features, cotangent, gate_weight, up_weight, gate_moment, up_moment)]
    nbits = lax.axis_size("rep").bit_length() - 1
    branches = [functools.partial(step_call, 2**bit) for bit in range(nbits)]
    results = lax.switch(step_index % nbits, branches, *arrays)
    return tuple(result[None] for result in results)


def solution(mesh):
    split = P("rep", "fsdp", None)
    return jax.shard_map(
        body, mesh=mesh, in_specs=(split,) * 6 + (P(),), out_specs=(split,) * 4, check_vma=False
    )
```

time: 497 us -> 98.5 us (0.20)
  waiting for transfers between devices: 428 us -> 0 us
  Pallas kernels: 0 us -> 94 us
  matrix products: 30.3 us -> 0 us
  between operations: 14.6 us -> 1.3 us
  other arithmetic: 11.7 us -> 0 us
  local copies, waits for them, and re-layouts: 10.7 us -> 2.83 us
    unnamed x4 -> x0, waiting for transfers between devices: 226 us -> none
    all_gather x2 -> x0, waiting for transfers between devices: 200 us -> none  [the longest x1 111 us: body(): lax.all_gather(local_gate, 'fsdp', axis=0, tiled=True)]
    pallas_call x0 -> x1, Pallas kernels: none -> 94 us  [step_call(): pl.pallas_call(functools.partial(step_kernel, stride), out_shape=(out,) *...]
    dot_general x3 -> x0, matrix products: 30.3 us -> none  [the longest x1 15.7 us: body(): lax.dot_general(gate_diff, local_feat, (((0,), (0,)), ((), ())), preferre...]
    unnamed x1 -> x0, other arithmetic: 8.25 us -> none
    unnamed x17 -> x4, local copies, waits for them, and re-layouts: 9.9 us -> 2.83 us
  transfers between devices with their start and end apart: 4 -> 0, of which waited for: 4 -> 0; matrix products, arithmetic and copies ran while one was open for 3% -> 0% of each run, Pallas kernels for 0% -> 0%
where the time goes in v1:
time: 98.5 us; the launch traced here: 98.1 us
  Pallas kernels  94 us (95%)
  local copies, waits for them, and re-layouts  2.83 us (3%)
  between operations  1.3 us (1%)
    pallas_call x1, Pallas kernels, step_call(): pl.pallas_call(functools.partial(step_kernel, stride), out_shape=(out,) *...  94 us
    unnamed x4, local copies, waits for them, and re-layouts  2.83 us

profile of v1, /device:TPU:0, one launch (start us, length us, event | category | flops | bytes accessed | tf_op | source)
XLA Modules:
  0.0 98.1 jit_solution(10007835285534969116)
XLA Ops:
  1.3 94.0 %conditional.1 = ((bf16[152,896]{1,0:T(8,128)(2,1)S(1)}, bf16[152,896]{1,0:T(8,128)(2,1)S(1)}, bf16[152,896]{1,0:T(8,128)(2,1)S(1)}, bf16[152,896]{1,0:T(8,128)(2,1)S(1)})) conditional(s32[]{:T(128)} %clamp.3, (bf16[384,896]{1,0:T(8,128)(2,1)}, bf16[384,4864]{1,0:T(8,128)(2,1)}, bf16[152,896]{1,0:T(8,128)(2,1)}, bf16[152,896]{1,0:T(8,128)(2,1)}, ...), branch_computations={%region_0.1_spmd, %region_1.2_spmd} | conditional | flops 13388218368 | bytes 4423688 | solution.py:369
  1.3 94.0 %step_stride_2.1 = (bf16[152,896]{1,0:T(8,128)(2,1)S(1)}, bf16[152,896]{1,0:T(8,128)(2,1)S(1)}, bf16[152,896]{1,0:T(8,128)(2,1)S(1)}, bf16[152,896]{1,0:T(8,128)(2,1)S(1)}) custom-call(bf16[384,896]{1,0:T(8,128)(2,1)} %get-tuple-element.46.feat_hbm, bf16[384,4864]{1,0:T(8,128)(2,1)} %get-tuple-element.47.cot_hbm, ...), custom_call_target="tpu_custom_call" | custom-call | flops 13388218368 | bytes 4423680 | tf_op jit(solution)/shard_map/cond/branch_1_fun/step_stride_2/pallas_call | solution.py:320
  95.3 0.7 copy.24
  96.0 0.7 copy.25
  96.7 0.7 copy.26
  97.4 0.7 copy.27

commit v2 on v0

v2 whole, which is shorter than its diff:
```python
import functools

import jax
import jax.numpy as jnp
from jax import lax
from jax.experimental import pallas as pl
from jax.experimental.pallas import tpu as pltpu
from jax.sharding import PartitionSpec as P

MESH = pl.DeviceIdType.MESH
F32 = jnp.float32
BF16 = jnp.bfloat16
MOMENT_DECAY = 0.9
STEP_RATE = 0.5

NX, NY, NZ = 4, 2, 4
FAR, FAR_MATE, NEXT, NEXT_MATE, BACK, BACK_MATE, OWN, OWN_MATE = (2, 0), (2, 1), (1, 0), (1, 1), (3, 0), (3, 1), (0, 0), (0, 1)
SLOT = {place: i for i, place in enumerate((FAR_MATE, NEXT_MATE, BACK_MATE, FAR, OWN_MATE, NEXT, BACK, OWN))}
CHUNKS = (
    ((FAR_MATE, 0), (FAR_MATE, 1)),
    ((NEXT_MATE, 0), (BACK_MATE, 0)),
    ((NEXT_MATE, 1), (BACK_MATE, 1)),
    ((FAR, 0), (FAR, 1)),
    ((OWN_MATE, 0), (OWN_MATE, 1)),
    ((NEXT, 0), (BACK, 0)),
    ((NEXT, 1), (BACK, 1)),
    ((OWN, 0),),
    ((OWN, 1),),
)
PIECES = tuple(piece for chunk in CHUNKS for piece in chunk)
AHEAD = 6
SEMS = 96


def sizes(rows):
    first = (rows // 2 + 15) // 16 * 16
    return first, rows - first


def step_kernel(stride, feat_hbm, cot_hbm, gate_hbm, up_hbm, gmom_hbm, umom_hbm, *refs):
    new_gate, new_up, mom_gate, mom_up = refs[:4]
    (feat, raw, weights, moments, grad, send_sems, recv_sems, local_sem) = refs[4:12]
    turned, cots, terms, far, relay, sums, crossed, stepped, other = (refs[i : i + 2] for i in range(12, 30, 2))
    tok, width = feat_hbm.shape
    rows = gate_hbm.shape[0]
    size = sizes(rows)
    span = (pl.ds(0, size[0]), pl.ds(size[0], size[1]))
    half = tok // 2
    factor = width ** (-0.5)
    rep, place = lax.axis_index("rep"), lax.axis_index("fsdp")
    x, y, z = place // (NY * NZ), lax.rem(place // NZ, NY), lax.rem(place, NZ)

    def index_of(dx, dy, dz):
        return lax.rem(x + dx, NX) * (NY * NZ) + lax.rem(y + dy, NY) * NZ + lax.rem(z + dz, NZ)

    mate = (rep + 1 - 2 * lax.rem(rep, 2), place) if stride == 1 else (lax.rem(rep + 2, 4), place)
    across = (rep, index_of(0, 1, 0))
    along_x = {dx: (rep, index_of(dx, 0, 0)) for dx in (1, 2, 3)}
    along_z = {dz: (rep, index_of(0, 0, dz)) for dz in (1, 3)}
    sent = {}

    def send(name, src, dst, target):
        number = len(sent)
        sent[name] = pltpu.make_async_remote_copy(
            src_ref=src,
            dst_ref=dst,
            send_sem=send_sems.at[number],
            recv_sem=recv_sems.at[number],
            device_id=target,
            device_id_type=MESH,
        )
        sent[name].start()

    def arrive(*name):
        sent[name].wait_recv()

    barrier = pltpu.get_barrier_semaphore()
    greeted = [mate, across, *along_x.values(), *along_z.values()]
    for target in greeted:
        pl.semaphore_signal(barrier, inc=1, device_id=target, device_id_type=MESH)
    pl.semaphore_wait(barrier, len(greeted))

    own_weights = (gate_hbm, up_hbm)

    def send_features(dx, part):
        there = feat.at[pl.ds((NX - dx) * tok + part * half, half)]
        send(("feat", dx, part), feat_hbm.at[pl.ds(part * half, half)], there, along_x[dx])

    turn_copy = pltpu.make_async_copy(cot_hbm, raw, local_sem.at[0])
    turn_copy.start()
    for kind in (0, 1):
        for dz, what in ((1, kind), (3, 1 - kind)):
            send(("w", dz, what), own_weights[what], weights.at[SLOT[NZ - dz, 0], what], along_z[dz])
        send_features(1, kind)
        send_features(3, 1 - kind)
        send(("w", "y", kind), own_weights[kind], weights.at[SLOT[OWN_MATE], kind], across)
    local = [
        pltpu.make_async_copy(feat_hbm, feat.at[pl.ds(0, tok)], local_sem.at[1]),
        pltpu.make_async_copy(gate_hbm, weights.at[SLOT[OWN], 0], local_sem.at[2]),
        pltpu.make_async_copy(up_hbm, weights.at[SLOT[OWN], 1], local_sem.at[3]),
        pltpu.make_async_copy(gmom_hbm, moments.at[0], local_sem.at[4]),
        pltpu.make_async_copy(umom_hbm, moments.at[1], local_sem.at[5]),
    ]
    for item in local:
        item.start()

    turn_copy.wait()
    group = 16 * rows

    def turn(g, carry):
        flat = raw[:, pl.ds(pl.multiple_of(g * group, 128), group)].astype(F32).T
        for s in range(16):
            turned[0][g * 16 + s] = flat[s * rows : s * rows + size[0]].astype(BF16)
            turned[1][g * 16 + s] = flat[s * rows + size[0] : (s + 1) * rows].astype(BF16)
        return carry

    lax.fori_loop(0, raw.shape[1] // group, turn, 0)

    for dz, kind in ((1, 0), (3, 1)):
        arrive("w", dz, kind)
        send(("w on", kind), weights.at[SLOT[NZ - dz, 0], kind], weights.at[SLOT[FAR], kind], along_z[dz])
    for dx, part in ((1, 0), (3, 1)):
        arrive("feat", dx, part)
        source = feat.at[pl.ds((NX - dx) * tok + part * half, half)]
        send(("feat on", part), source, feat.at[pl.ds(2 * tok + part * half, half)], along_x[dx])
    for kind in (0, 1):
        arrive("w", "y", kind)
        for dz in (1, 3):
            source = weights.at[SLOT[OWN_MATE], kind]
            send(("w mate", dz, kind), source, weights.at[SLOT[NZ - dz, 1], kind], along_z[dz])

    started = [0]

    def send_cots(upto):
        for number in range(started[0], min(upto, len(PIECES))):
            (dz, dy), part = PIECES[number]
            for dx in (1, 3, 2):
                source = turned[part].at[index_of(dx, dy, dz)]
                there = cots[part].at[NX - dx - 1, SLOT[dz, dy]]
                send(("cot", dx, number), source, there, along_x[dx])
        started[0] = max(started[0], upto)

    send_cots(AHEAD)
    for kind in (0, 1):
        arrive("w on", kind)
        send(("w far", kind), weights.at[SLOT[FAR], kind], weights.at[SLOT[FAR_MATE], kind], across)
    for item in local:
        item.wait()
    arrive("feat", 1, 1)
    arrive("feat", 3, 0)
    arrive("feat on", 0)
    arrive("feat on", 1)

    def products(pieces):
        operand, diffs, top = [], [], 0
        for slot, part in pieces:
            operand += [weights[SLOT[slot], kind, span[part]].astype(F32) for kind in (0, 1)]
        operand = jnp.concatenate(operand, 0).astype(BF16)
        made = lax.dot_general(operand, feat[...], (((1,), (1,)), ((), ())), preferred_element_type=F32) * factor
        for (dz, dy), part in pieces:
            n = size[part]
            gate, upward = made[top : top + n], made[top + n : top + 2 * n]
            top += 2 * n
            blocks = [turned[part][index_of(0, dy, dz)]] + [cots[part][dx, SLOT[dz, dy]] for dx in range(NX - 1)]
            tangent = jnp.concatenate([block.astype(F32) for block in blocks], 1)
            sigma = jax.nn.sigmoid(gate)
            scaled = factor * tangent * sigma
            diffs += [scaled * upward * (1.0 + gate * (1.0 - sigma)), scaled * gate]
        diffs = jnp.concatenate(diffs, 0).astype(BF16)
        grad[pl.ds(0, top)] = jnp.dot(diffs, feat[...], preferred_element_type=F32)

    def sides(dy, part):
        arrive("term", 1, dy, part)
        arrive("term", 3, dy, part)
        return sums[part][0, dy].astype(F32) + sums[part][1, dy].astype(F32)

    def finish(part):
        value = grad[pl.ds(0, 2 * size[part])] + sides(0, part)
        arrive("cross", part)
        value = value + crossed[part][...].astype(F32)
        n = size[part]
        for kind, out in ((0, mom_gate), (1, mom_up)):
            here = pl.ds(kind * n, n)
            moment = MOMENT_DECAY * moments[kind, span[part]].astype(F32) + value[kind * n : (kind + 1) * n]
            moment = moment.astype(BF16)
            out[span[part]] = moment
            weight = weights[SLOT[OWN], kind, span[part]].astype(F32)
            stepped[part][here] = (weight - STEP_RATE * moment.astype(F32)).astype(BF16)
        send(("swap", part), stepped[part], other[part], mate)

    for order, pieces in enumerate(CHUNKS):
        for slot, part in pieces:
            dz, dy = slot
            if slot == FAR_MATE and part == 0:
                arrive("w far", 0)
                arrive("w far", 1)
            if slot in (NEXT_MATE, BACK_MATE) and part == 0:
                arrive("w mate", NZ - dz, 0)
                arrive("w mate", NZ - dz, 1)
            if slot in (NEXT, BACK) and part == 0:
                arrive("w", NZ - dz, 0 if dz == 1 else 1)
            number = PIECES.index((slot, part))
            for dx in (1, 3, 2):
                arrive("cot", dx, number)
        send_cots(2 * order + 2 + AHEAD)
        products(pieces)
        top = 0
        for slot, part in pieces:
            (dz, dy), n = slot, 2 * size[part]
            here = terms[part].at[SLOT[slot]]
            if slot == OWN:
                finish(part)
                continue
            term = grad[pl.ds(top, n)]
            top += n
            if slot == FAR_MATE:
                here[...] = term.astype(BF16)
                send(("far", part), here, far[part], across)
            elif slot == FAR:
                arrive("far", part)
                here[...] = (term + far[part][...].astype(F32)).astype(BF16)
                send(("relay", part), here, relay[part], along_z[1 if part == 0 else 3])
            elif slot == OWN_MATE:
                here[...] = (term + sides(1, part)).astype(BF16)
                send(("cross", part), here, crossed[part], across)
            else:
                if dy == 0 and part == (0 if dz == 1 else 1):
                    arrive("relay", part)
                    term = term + relay[part][...].astype(F32)
                here[...] = term.astype(BF16)
                send(("term", dz, dy, part), here, sums[part].at[dz // 2, dy], along_z[dz])

    for part in (0, 1):
        arrive("swap", part)
        average = (stepped[part][...].astype(F32) + other[part][...].astype(F32)) * 0.5
        n = size[part]
        new_gate[span[part]] = average[:n].astype(BF16)
        new_up[span[part]] = average[n:].astype(BF16)

    for item in sent.values():
        item.wait_send()


def step_call(stride, features, cotangent, gate_weight, up_weight, gate_moment, up_moment):
    tok, width = features.shape
    rows = gate_weight.shape[0]
    hidden = cotangent.shape[1]
    slots = hidden // rows
    size = sizes(rows)
    dma = pltpu.SemaphoreType.DMA
    out = jax.ShapeDtypeStruct((rows, width), BF16)

    def parts(*lead, of=2, last=width):
        return [pltpu.VMEM((*lead, of * n, last), BF16) for n in size]

    return pl.pallas_call(
        functools.partial(step_kernel, stride),
        out_shape=(out,) * 4,
        in_specs=[pl.BlockSpec(memory_space=pl.ANY)] * 6,
        out_specs=(pl.BlockSpec(memory_space=pltpu.VMEM),) * 4,
        scratch_shapes=[
            pltpu.VMEM((NX * tok, width), BF16),
            pltpu.VMEM((tok, hidden), BF16),
            pltpu.VMEM((NY * NZ, 2, rows, width), BF16),
            pltpu.VMEM((2, rows, width), BF16),
            pltpu.VMEM((4 * size[0], width), F32),
            dma((SEMS,)),
            dma((SEMS,)),
            dma((6,)),
            *parts(slots, of=1, last=tok),
            *parts(NX - 1, NY * NZ, of=1, last=tok),
            *parts(NY * NZ - 1),
            *parts(),
            *parts(),
            *parts(2, 2),
            *parts(),
            *parts(),
            *parts(),
        ],
        compiler_params=pltpu.CompilerParams(
            collective_id=stride - 1, has_side_effects=True, vmem_limit_bytes=56 * 2**20
        ),
        cost_estimate=pl.CostEstimate(
            flops=8 * tok * hidden * width, bytes_accessed=2 * tok * (hidden + width), transcendentals=tok * hidden
        ),
        name=f"step_stride_{stride}",
    )(features, cotangent, gate_weight, up_weight, gate_moment, up_moment)


def store_kernel(*refs):
    sources, targets, sem = refs[:4], refs[4:8], refs[8]
    copies = [pltpu.make_async_copy(s, t, sem.at[i]) for i, (s, t) in enumerate(zip(sources, targets))]
    for item in copies:
        item.start()
    for item in copies:
        item.wait()


def store(arrays):
    return pl.pallas_call(
        store_kernel,
        out_shape=tuple(jax.ShapeDtypeStruct(a.shape, a.dtype) for a in arrays),
        in_specs=[pl.BlockSpec(memory_space=pltpu.VMEM)] * 4,
        out_specs=(pl.BlockSpec(memory_space=pl.ANY),) * 4,
        scratch_shapes=[pltpu.SemaphoreType.DMA((4,))],
        name="store",
    )(*arrays)


def body(features, cotangent, gate_weight, up_weight, gate_moment, up_moment, step_index):
    arrays = [a[0] for a in (features, cotangent, gate_weight, up_weight, gate_moment, up_moment)]
    nbits = lax.axis_size("rep").bit_length() - 1
    branches = [functools.partial(step_call, 2**bit) for bit in range(nbits)]
    results = store(lax.switch(step_index % nbits, branches, *arrays))
    return tuple(result[None] for result in results)


def solution(mesh):
    split = P("rep", "fsdp", None)
    return jax.shard_map(
        body, mesh=mesh, in_specs=(split,) * 6 + (P(),), out_specs=(split,) * 4, check_vma=False
    )
```

time: 497 us -> 89.6 us (0.18)
  waiting for transfers between devices: 428 us -> 0 us
  Pallas kernels: 0 us -> 87.4 us
  matrix products: 30.3 us -> 0 us
  between operations: 14.6 us -> 1.52 us
  other arithmetic: 11.7 us -> 0 us
  local copies, waits for them, and re-layouts: 10.7 us -> 0 us
    unnamed x4 -> x0, waiting for transfers between devices: 226 us -> none
    all_gather x2 -> x0, waiting for transfers between devices: 200 us -> none  [the longest x1 111 us: body(): lax.all_gather(local_gate, 'fsdp', axis=0, tiled=True)]
    pallas_call x0 -> x2, Pallas kernels: none -> 87.4 us  [the longest x1 86.4 us: step_call(): pl.pallas_call(functools.partial(step_kernel, stride), out_shape=(out,) *...]
    dot_general x3 -> x0, matrix products: 30.3 us -> none  [the longest x1 15.7 us: body(): lax.dot_general(gate_diff, local_feat, (((0,), (0,)), ((), ())), preferre...]
    unnamed x17 -> x0, local copies, waits for them, and re-layouts: 9.9 us -> none
    unnamed x1 -> x0, other arithmetic: 8.25 us -> none
  transfers between devices with their start and end apart: 4 -> 0, of which waited for: 4 -> 0; matrix products, arithmetic and copies ran while one was open for 3% -> 0% of each run, Pallas kernels for 0% -> 0%
where the time goes in v2:
time: 89.6 us; the launch traced here: 89.5 us
  Pallas kernels  87.4 us (98%)
  between operations  1.52 us (2%)
    pallas_call x1, Pallas kernels, step_call(): pl.pallas_call(functools.partial(step_kernel, stride), out_shape=(out,) *...  86.4 us

profile of v2, /device:TPU:0, one launch (start us, length us, event | category | flops | bytes accessed | tf_op | source)
XLA Modules:
  0.0 89.5 jit_solution(1531664555881968752)
XLA Ops:
  1.3 87.0 %conditional.1 = ((bf16[152,896]{1,0:T(8,128)(2,1)S(1)}, bf16[152,896]{1,0:T(8,128)(2,1)S(1)}, bf16[152,896]{1,0:T(8,128)(2,1)S(1)}, bf16[152,896]{1,0:T(8,128)(2,1)S(1)})) conditional(s32[]{:T(128)} %clamp.3, (bf16[384,896]{1,0:T(8,128)(2,1)}, bf16[384,4864]{1,0:T(8,128)(2,1)}, bf16[152,896]{1,0:T(8,128)(2,1)}, bf16[152,896]{1,0:T(8,128)(2,1)}, ...), branch_computations={%region_0.1_spmd, %region_1.2_spmd} | conditional | flops 13388218368 | bytes 4423688 | solution.py:314
  1.5 86.4 %step_stride_2.1 = (bf16[152,896]{1,0:T(8,128)(2,1)S(1)}, bf16[152,896]{1,0:T(8,128)(2,1)S(1)}, bf16[152,896]{1,0:T(8,128)(2,1)S(1)}, bf16[152,896]{1,0:T(8,128)(2,1)S(1)}) custom-call(bf16[384,896]{1,0:T(8,128)(2,1)} %get-tuple-element.30.feat_hbm, bf16[384,4864]{1,0:T(8,128)(2,1)} %get-tuple-element.31.cot_hbm, ...), custom_call_target="tpu_custom_call" | custom-call | flops 13388218368 | bytes 4423680 | tf_op jit(solution)/shard_map/cond/branch_1_fun/step_stride_2/pallas_call | solution.py:256
  88.3 1.0 %store.1 = (bf16[152,896]{1,0:T(8,128)(2,1)}, bf16[152,896]{1,0:T(8,128)(2,1)}, bf16[152,896]{1,0:T(8,128)(2,1)}, bf16[152,896]{1,0:T(8,128)(2,1)}) custom-call(bf16[152,896]{1,0:T(8,128)(2,1)S(1)} %get-tuple-element.48.refs_0_, bf16[152,896]{1,0:T(8,128)(2,1)S(1)} %get-tuple-element.49.refs_1_, bf16[152,896]{1,0:T(8,128)(2,1)S(1)} %get-tuple-element.50.refs_2_, ...), custom_call_target="tpu_custom_call" | custom-call | tf_op jit(solution)/shard_map/store/pallas_call | solution.py:300

commit v3 on v2

v3 whole, which is shorter than its diff:
```python
import functools

import jax
import jax.numpy as jnp
from jax import lax
from jax.experimental import pallas as pl
from jax.experimental.pallas import tpu as pltpu
from jax.sharding import PartitionSpec as P

MESH = pl.DeviceIdType.MESH
F32 = jnp.float32
BF16 = jnp.bfloat16
MOMENT_DECAY = 0.9
STEP_RATE = 0.5

NX, NY, NZ = 4, 2, 4
PLACES = {
    "far": (2, 0),
    "far mate": (2, 1),
    "next": (1, 0),
    "next mate": (1, 1),
    "back": (3, 0),
    "back mate": (3, 1),
    "own": (0, 0),
    "own mate": (0, 1),
}
FAR, FAR_MATE, NEXT, NEXT_MATE, BACK, BACK_MATE, OWN, OWN_MATE = PLACES.values()
SLOT = {place: i for i, place in enumerate((FAR_MATE, NEXT_MATE, BACK_MATE, FAR, OWN_MATE, NEXT, BACK, OWN))}
ORDERS = {
    1: (
        ("back mate", 1), ("next mate", 0), ("far mate", 0), ("back mate", 0), ("next mate", 1), ("far mate", 1), ("far", 0), ("back", 0),
        ("far", 1), ("own mate", 1), ("next", 0), ("own mate", 0), ("back", 1), ("next", 1), ("own", 0), ("own", 1),
    ),
    2: (
        ("next mate", 1), ("back", 0), ("next mate", 0), ("far mate", 0), ("back mate", 0), ("far mate", 1), ("far", 0), ("back mate", 1),
        ("own mate", 0), ("far", 1), ("next", 0), ("own mate", 1), ("next", 1), ("own", 0), ("back", 1), ("own", 1),
    ),
}
ORDERS = {stride: tuple((PLACES[name], part) for name, part in order) for stride, order in ORDERS.items()}
AHEAD = 6


def sizes(rows):
    first = (rows // 2 + 15) // 16 * 16
    return first, rows - first


def choose(values, index):
    result = values[0]
    for number, value in enumerate(values[1:], 1):
        result = jnp.where(index == number, value, result)
    return result


def step_kernel(stride, feat_hbm, cot_hbm, gate_hbm, up_hbm, gmom_hbm, umom_hbm, *refs):
    new_gate, new_up, mom_gate, mom_up = refs[:4]
    (feat, raw, weights, moments, grad, send_sems, recv_sems, local_sem) = refs[4:12]
    n_parts = len(sizes(gate_hbm.shape[0]))
    turned, cots, terms, far, relay, sums, crossed, stepped, other = (
        refs[12 + i * n_parts : 12 + (i + 1) * n_parts] for i in range(9)
    )
    pieces = ORDERS[stride]
    tok, width = feat_hbm.shape
    rows = gate_hbm.shape[0]
    size = sizes(rows)
    first = [sum(size[:part]) for part in range(n_parts)]
    span = [pl.ds(first[part], size[part]) for part in range(n_parts)]
    half = tok // 2
    factor = width ** (-0.5)
    rep, place = lax.axis_index("rep"), lax.axis_index("fsdp")
    x, y, z = place // (NY * NZ), lax.rem(place // NZ, NY), lax.rem(place, NZ)

    def index_of(dx, dy, dz):
        return lax.rem(x + dx, NX) * (NY * NZ) + lax.rem(y + dy, NY) * NZ + lax.rem(z + dz, NZ)

    mate = (rep + 1 - 2 * lax.rem(rep, 2), place) if stride == 1 else (lax.rem(rep + 2, 4), place)
    across = (rep, index_of(0, 1, 0))
    along_x = {dx: (rep, index_of(dx, 0, 0)) for dx in (1, 2, 3)}
    along_z = {dz: (rep, index_of(0, 0, dz)) for dz in (1, 3)}
    sent = {}

    def relayed(part):
        return 1 if part % 2 == 0 else 3

    def plan(name, src, dst, target):
        number = len(sent)
        sent[name] = pltpu.make_async_remote_copy(
            src_ref=src,
            dst_ref=dst,
            send_sem=send_sems.at[number],
            recv_sem=recv_sems.at[number],
            device_id=target,
            device_id_type=MESH,
        )

    def go(*name):
        sent[name].start()

    def send(name, src, dst, target):
        plan(name, src, dst, target)
        go(*name)

    arrived = set()

    def arrive(*name):
        if name not in arrived:
            arrived.add(name)
            sent[name].wait_recv()

    barrier = pltpu.get_barrier_semaphore()
    greeted = [mate, across, *along_x.values(), *along_z.values()]
    for target in greeted:
        pl.semaphore_signal(barrier, inc=1, device_id=target, device_id_type=MESH)
    pl.semaphore_wait(barrier, len(greeted))

    own_weights = (gate_hbm, up_hbm)

    def send_features(dx, part):
        there = feat.at[pl.ds((NX - dx) * tok + part * half, half)]
        send(("feat", dx, part), feat_hbm.at[pl.ds(part * half, half)], there, along_x[dx])

    turn_copy = pltpu.make_async_copy(cot_hbm, raw, local_sem.at[0])
    turn_copy.start()
    for kind in (0, 1):
        for dz, what in ((1, kind), (3, 1 - kind)):
            send(("w", dz, what), own_weights[what], weights.at[SLOT[NZ - dz, 0], what], along_z[dz])
        send_features(1, kind)
        send_features(3, 1 - kind)
        send(("w", "y", kind), own_weights[kind], weights.at[SLOT[OWN_MATE], kind], across)
    local = [
        pltpu.make_async_copy(feat_hbm, feat.at[pl.ds(0, tok)], local_sem.at[1]),
        pltpu.make_async_copy(gate_hbm, weights.at[SLOT[OWN], 0], local_sem.at[2]),
        pltpu.make_async_copy(up_hbm, weights.at[SLOT[OWN], 1], local_sem.at[3]),
        pltpu.make_async_copy(gmom_hbm, moments.at[0], local_sem.at[4]),
        pltpu.make_async_copy(umom_hbm, moments.at[1], local_sem.at[5]),
    ]
    for item in local:
        item.start()

    turn_copy.wait()
    group = 16 * rows

    def turn(g, carry):
        flat = raw[:, pl.ds(pl.multiple_of(g * group, 128), group)].astype(F32).T
        for s in range(16):
            for part in range(n_parts):
                top = s * rows + first[part]
                turned[part][g * 16 + s] = flat[top : top + size[part]].astype(BF16)
        return carry

    lax.fori_loop(0, raw.shape[1] // group, turn, 0)

    for dz, kind in ((1, 0), (3, 1)):
        arrive("w", dz, kind)
        send(("w on", kind), weights.at[SLOT[NZ - dz, 0], kind], weights.at[SLOT[FAR], kind], along_z[dz])
    for dx, part in ((1, 0), (3, 1)):
        arrive("feat", dx, part)
        source = feat.at[pl.ds((NX - dx) * tok + part * half, half)]
        send(("feat on", part), source, feat.at[pl.ds(2 * tok + part * half, half)], along_x[dx])
    for kind in (0, 1):
        arrive("w", "y", kind)
        for dz in (1, 3):
            source = weights.at[SLOT[OWN_MATE], kind]
            send(("w mate", dz, kind), source, weights.at[SLOT[NZ - dz, 1], kind], along_z[dz])

    for number, ((dz, dy), part) in enumerate(pieces):
        for dx in (1, 3, 2):
            source = turned[part].at[index_of(dx, dy, dz)]
            plan(("cot", dx, number), source, cots[part].at[NX - dx - 1, SLOT[dz, dy]], along_x[dx])
    for slot, part in pieces:
        dz, dy = slot
        here = None if slot == OWN else terms[part].at[SLOT[slot]]
        if slot == FAR_MATE:
            plan(("far", part), here, far[part], across)
        elif slot == FAR:
            plan(("relay", part), here, relay[part], along_z[relayed(part)])
        elif slot == OWN_MATE:
            plan(("cross", part), here, crossed[part], across)
        elif slot == OWN:
            plan(("swap", part), stepped[part], other[part], mate)
        else:
            plan(("term", dz, dy, part), here, sums[part].at[dz // 2, dy], along_z[dz])

    def send_cots(number):
        if number < len(pieces):
            for dx in (1, 3, 2):
                go("cot", dx, number)

    for number in range(AHEAD):
        send_cots(number)
    for kind in (0, 1):
        arrive("w on", kind)
        send(("w far", kind), weights.at[SLOT[FAR], kind], weights.at[SLOT[FAR_MATE], kind], across)
    for item in local:
        item.wait()
    arrive("feat", 1, 1)
    arrive("feat", 3, 0)
    arrive("feat on", 0)
    arrive("feat on", 1)

    def products(part, slot, own):
        n = size[part]
        both = [weights[slot, kind, span[part]].astype(F32) for kind in (0, 1)]
        both = jnp.concatenate(both, 0).astype(BF16)
        made = lax.dot_general(both, feat[...], (((1,), (1,)), ((), ())), preferred_element_type=F32) * factor
        gate, upward = made[:n], made[n:]
        blocks = [turned[part][own]] + [cots[part][dx, slot] for dx in range(NX - 1)]
        tangent = jnp.concatenate([block.astype(F32) for block in blocks], 1)
        sigma = jax.nn.sigmoid(gate)
        scaled = factor * tangent * sigma
        diffs = [scaled * upward * (1.0 + gate * (1.0 - sigma)), scaled * gate]
        diffs = jnp.concatenate(diffs, 0).astype(BF16)
        grad[pl.ds(0, 2 * n)] = jnp.dot(diffs, feat[...], preferred_element_type=F32)

    def sides(dy, part):
        arrive("term", 1, dy, part)
        arrive("term", 3, dy, part)
        return sums[part][0, dy].astype(F32) + sums[part][1, dy].astype(F32)

    def finish(part):
        n = size[part]
        value = grad[pl.ds(0, 2 * n)] + sides(0, part)
        arrive("cross", part)
        value = value + crossed[part][...].astype(F32)
        for kind, out in ((0, mom_gate), (1, mom_up)):
            moment = MOMENT_DECAY * moments[kind, span[part]].astype(F32) + value[kind * n : (kind + 1) * n]
            moment = moment.astype(BF16)
            out[span[part]] = moment
            weight = weights[SLOT[OWN], kind, span[part]].astype(F32)
            stepped[part][pl.ds(kind * n, n)] = (weight - STEP_RATE * moment.astype(F32)).astype(BF16)
        go("swap", part)

    slots = [SLOT[slot] for slot, part in pieces]
    owns = [index_of(0, dy, dz) for (dz, dy), part in pieces]

    def work(index, carry):
        for number, (slot, part) in enumerate(pieces):

            @pl.when(index == number)
            def _():
                dz, dy = slot
                for name in {
                    FAR_MATE: (("w far", 0), ("w far", 1)),
                    NEXT_MATE: (("w mate", 3, 0), ("w mate", 3, 1)),
                    BACK_MATE: (("w mate", 1, 0), ("w mate", 1, 1)),
                    NEXT: (("w", 3, 0),),
                    BACK: (("w", 1, 1),),
                }.get(slot, ()):
                    arrive(*name)
                for dx in (1, 3, 2):
                    arrive("cot", dx, number)
                send_cots(number + AHEAD)

        slot_here, own_here = choose(slots, index), choose(owns, index)
        part_here = choose([part for slot, part in pieces], index)
        for part in range(n_parts):

            @pl.when(part_here == part)
            def _():
                products(part, slot_here, own_here)

        for number, (slot, part) in enumerate(pieces):

            @pl.when(index == number)
            def _():
                dz, dy = slot
                if slot == OWN:
                    finish(part)
                    return
                term = grad[pl.ds(0, 2 * size[part])]
                name = ("term", dz, dy, part)
                if slot == FAR_MATE:
                    name = ("far", part)
                elif slot == FAR:
                    name = ("relay", part)
                    arrive("far", part)
                    term = term + far[part][...].astype(F32)
                elif slot == OWN_MATE:
                    name = ("cross", part)
                    term = term + sides(1, part)
                elif dy == 0 and dz == relayed(part):
                    arrive("relay", part)
                    term = term + relay[part][...].astype(F32)
                terms[part][SLOT[slot]] = term.astype(BF16)
                go(*name)

        return carry

    lax.fori_loop(0, len(pieces), work, 0)

    for part in range(n_parts):
        arrive("swap", part)
        average = (stepped[part][...].astype(F32) + other[part][...].astype(F32)) * 0.5
        n = size[part]
        new_gate[span[part]] = average[:n].astype(BF16)
        new_up[span[part]] = average[n:].astype(BF16)

    for item in sent.values():
        item.wait_send()


def step_call(stride, features, cotangent, gate_weight, up_weight, gate_moment, up_moment):
    tok, width = features.shape
    rows = gate_weight.shape[0]
    hidden = cotangent.shape[1]
    slots = hidden // rows
    size = sizes(rows)
    sems = 20 + 32 * len(size)
    dma = pltpu.SemaphoreType.DMA
    out = jax.ShapeDtypeStruct((rows, width), BF16)

    def parts(*lead, of=2, last=width):
        return [pltpu.VMEM((*lead, of * n, last), BF16) for n in size]

    return pl.pallas_call(
        functools.partial(step_kernel, stride),
        out_shape=(out,) * 4,
        in_specs=[pl.BlockSpec(memory_space=pl.ANY)] * 6,
        out_specs=(pl.BlockSpec(memory_space=pltpu.VMEM),) * 4,
        scratch_shapes=[
            pltpu.VMEM((NX * tok, width), BF16),
            pltpu.VMEM((tok, hidden), BF16),
            pltpu.VMEM((NY * NZ, 2, rows, width), BF16),
            pltpu.VMEM((2, rows, width), BF16),
            pltpu.VMEM((2 * max(size), width), F32),
            dma((sems,)),
            dma((sems,)),
            dma((6,)),
            *parts(slots, of=1, last=tok),
            *parts(NX - 1, NY * NZ, of=1, last=tok),
            *parts(NY * NZ - 1),
            *parts(),
            *parts(),
            *parts(2, 2),
            *parts(),
            *parts(),
            *parts(),
        ],
        compiler_params=pltpu.CompilerParams(
            collective_id=stride - 1, has_side_effects=True, vmem_limit_bytes=56 * 2**20
        ),
        cost_estimate=pl.CostEstimate(
            flops=8 * tok * hidden * width, bytes_accessed=2 * tok * (hidden + width), transcendentals=tok * hidden
        ),
        name=f"step_stride_{stride}",
    )(features, cotangent, gate_weight, up_weight, gate_moment, up_moment)


def store_kernel(*refs):
    sources, targets, sem = refs[:4], refs[4:8], refs[8]
    copies = [pltpu.make_async_copy(s, t, sem.at[i]) for i, (s, t) in enumerate(zip(sources, targets))]
    for item in copies:
        item.start()
    for item in copies:
        item.wait()


def store(arrays):
    return pl.pallas_call(
        store_kernel,
        out_shape=tuple(jax.ShapeDtypeStruct(a.shape, a.dtype) for a in arrays),
        in_specs=[pl.BlockSpec(memory_space=pltpu.VMEM)] * 4,
        out_specs=(pl.BlockSpec(memory_space=pl.ANY),) * 4,
        scratch_shapes=[pltpu.SemaphoreType.DMA((4,))],
        name="store",
    )(*arrays)


def body(features, cotangent, gate_weight, up_weight, gate_moment, up_moment, step_index):
    arrays = [a[0] for a in (features, cotangent, gate_weight, up_weight, gate_moment, up_moment)]
    nbits = lax.axis_size("rep").bit_length() - 1
    branches = [functools.partial(step_call, 2**bit) for bit in range(nbits)]
    results = store(lax.switch(lax.rem(step_index, nbits), branches, *arrays))
    return tuple(result[None] for result in results)


def solution(mesh):
    split = P("rep", "fsdp", None)
    return jax.shard_map(
        body, mesh=mesh, in_specs=(split,) * 6 + (P(),), out_specs=(split,) * 4, check_vma=False
    )
```

time: 89.6 us -> 88.1 us (0.983)
  Pallas kernels: 87.4 us -> 85.7 us
    pallas_call x1, Pallas kernels: 86.4 us -> 84.7 us  [step_call(): pl.pallas_call(functools.partial(step_kernel, stride), out_shape=(out,) *...]
where the time goes in v3:
time: 88.1 us; the launch traced here: 87.4 us
  Pallas kernels  85.7 us (97%)
  between operations  1.46 us (2%)
    pallas_call x1, Pallas kernels, step_call(): pl.pallas_call(functools.partial(step_kernel, stride), out_shape=(out,) *...  84.7 us

profile of v3, /device:TPU:0, one launch (start us, length us, event | category | flops | bytes accessed | tf_op | source)
XLA Modules:
  0.0 87.4 jit_solution(12245046621753102677)
XLA Ops:
  1.3 84.9 %conditional.1 = ((bf16[152,896]{1,0:T(8,128)(2,1)S(1)}, bf16[152,896]{1,0:T(8,128)(2,1)S(1)}, bf16[152,896]{1,0:T(8,128)(2,1)S(1)}, bf16[152,896]{1,0:T(8,128)(2,1)S(1)})) conditional(s32[]{:T(128)} %clamp.3, (bf16[384,896]{1,0:T(8,128)(2,1)}, bf16[384,4864]{1,0:T(8,128)(2,1)}, bf16[152,896]{1,0:T(8,128)(2,1)}, bf16[152,896]{1,0:T(8,128)(2,1)}, ...), branch_computations={%region_0.0_spmd, %region_1.0_spmd} | conditional | flops 13388218368 | bytes 4423688 | solution.py:373
  1.5 84.7 %step_stride_2.1 = (bf16[152,896]{1,0:T(8,128)(2,1)S(1)}, bf16[152,896]{1,0:T(8,128)(2,1)S(1)}, bf16[152,896]{1,0:T(8,128)(2,1)S(1)}, bf16[152,896]{1,0:T(8,128)(2,1)S(1)}) custom-call(bf16[384,896]{1,0:T(8,128)(2,1)} %get-tuple-element.30.feat_hbm, bf16[384,4864]{1,0:T(8,128)(2,1)} %get-tuple-element.31.cot_hbm, ...), custom_call_target="tpu_custom_call" | custom-call | flops 13388218368 | bytes 4423680 | tf_op jit(solution)/shard_map/cond/branch_1_fun/step_stride_2/pallas_call | solution.py:315
  86.2 1.0 %store.1 = (bf16[152,896]{1,0:T(8,128)(2,1)}, bf16[152,896]{1,0:T(8,128)(2,1)}, bf16[152,896]{1,0:T(8,128)(2,1)}, bf16[152,896]{1,0:T(8,128)(2,1)}) custom-call(bf16[152,896]{1,0:T(8,128)(2,1)S(1)} %get-tuple-element.48.refs_0_, bf16[152,896]{1,0:T(8,128)(2,1)S(1)} %get-tuple-element.49.refs_1_, bf16[152,896]{1,0:T(8,128)(2,1)S(1)} %get-tuple-element.50.refs_2_, ...), custom_call_target="tpu_custom_call" | custom-call | tf_op jit(solution)/shard_map/store/pallas_call | solution.py:359

commit v4 on v3

--- a/solution.py
+++ b/solution.py
@@ -28,12 +28,12 @@
 SLOT = {place: i for i, place in enumerate((FAR_MATE, NEXT_MATE, BACK_MATE, FAR, OWN_MATE, NEXT, BACK, OWN))}
 ORDERS = {
     1: (
-        ("back mate", 1), ("next mate", 0), ("far mate", 0), ("back mate", 0), ("next mate", 1), ("far mate", 1), ("far", 0), ("back", 0),
-        ("far", 1), ("own mate", 1), ("next", 0), ("own mate", 0), ("back", 1), ("next", 1), ("own", 0), ("own", 1),
+        ("next mate", 0), ("back mate", 0), ("far mate", 0), ("back mate", 1), ("next mate", 1), ("far mate", 1), ("far", 0), ("back", 0),
+        ("own mate", 0), ("next", 0), ("far", 1), ("own mate", 1), ("next", 1), ("back", 1), ("own", 0), ("own", 1),
     ),
     2: (
-        ("next mate", 1), ("back", 0), ("next mate", 0), ("far mate", 0), ("back mate", 0), ("far mate", 1), ("far", 0), ("back mate", 1),
-        ("own mate", 0), ("far", 1), ("next", 0), ("own mate", 1), ("next", 1), ("own", 0), ("back", 1), ("own", 1),
+        ("next mate", 0), ("far mate", 0), ("back mate", 0), ("next mate", 1), ("back", 0), ("far mate", 1), ("far", 0), ("own mate", 0),
+        ("back mate", 1), ("next", 0), ("far", 1), ("own mate", 1), ("own", 0), ("next", 1), ("back", 1), ("own", 1),
     ),
 }
 ORDERS = {stride: tuple((PLACES[name], part) for name, part in order) for stride, order in ORDERS.items()}
@@ -41,7 +41,7 @@
 
 
 def sizes(rows):
-    first = (rows // 2 + 15) // 16 * 16
+    first = rows * 96 // 152 // 16 * 16
     return first, rows - first
 
 
@@ -120,13 +120,14 @@
         send(("feat", dx, part), feat_hbm.at[pl.ds(part * half, half)], there, along_x[dx])
 
     turn_copy = pltpu.make_async_copy(cot_hbm, raw, local_sem.at[0])
-    turn_copy.start()
     for kind in (0, 1):
+        send_features(1, kind)
+        send_features(3, 1 - kind)
         for dz, what in ((1, kind), (3, 1 - kind)):
             send(("w", dz, what), own_weights[what], weights.at[SLOT[NZ - dz, 0], what], along_z[dz])
-        send_features(1, kind)
-        send_features(3, 1 - kind)
         send(("w", "y", kind), own_weights[kind], weights.at[SLOT[OWN_MATE], kind], across)
+        if kind == 0:
+            turn_copy.start()
     local = [
         pltpu.make_async_copy(feat_hbm, feat.at[pl.ds(0, tok)], local_sem.at[1]),
         pltpu.make_async_copy(gate_hbm, weights.at[SLOT[OWN], 0], local_sem.at[2]),
@@ -288,6 +289,9 @@
 
     lax.fori_loop(0, len(pieces), work, 0)
 
+    for name, item in sent.items():
+        if name[0] != "swap":
+            item.wait_send()
     for part in range(n_parts):
         arrive("swap", part)
         average = (stepped[part][...].astype(F32) + other[part][...].astype(F32)) * 0.5
@@ -295,8 +299,8 @@
         new_gate[span[part]] = average[:n].astype(BF16)
         new_up[span[part]] = average[n:].astype(BF16)
 
-    for item in sent.values():
-        item.wait_send()
+    for part in range(n_parts):
+        sent["swap", part].wait_send()
 
 
 def step_call(stride, features, cotangent, gate_weight, up_weight, gate_moment, up_moment):

time: 88.1 us -> 86.5 us (0.982)
  Pallas kernels: 85.7 us -> 84.7 us
    pallas_call x1, Pallas kernels: 84.7 us -> 83.7 us  [step_call(): pl.pallas_call(functools.partial(step_kernel, stride), out_shape=(out,) *...]
where the time goes in v4:
time: 86.5 us; the launch traced here: 86.3 us
  Pallas kernels  84.7 us (98%)
  between operations  1.46 us (2%)
    pallas_call x1, Pallas kernels, step_call(): pl.pallas_call(functools.partial(step_kernel, stride), out_shape=(out,) *...  83.7 us

profile of v4, /device:TPU:0, one launch (start us, length us, event | category | flops | bytes accessed | tf_op | source)
XLA Modules:
  0.0 86.3 jit_solution(2332291401555498808)
XLA Ops:
  1.3 83.9 %conditional.1 = ((bf16[152,896]{1,0:T(8,128)(2,1)S(1)}, bf16[152,896]{1,0:T(8,128)(2,1)S(1)}, bf16[152,896]{1,0:T(8,128)(2,1)S(1)}, bf16[152,896]{1,0:T(8,128)(2,1)S(1)})) conditional(s32[]{:T(128)} %clamp.3, (bf16[384,896]{1,0:T(8,128)(2,1)}, bf16[384,4864]{1,0:T(8,128)(2,1)}, bf16[152,896]{1,0:T(8,128)(2,1)}, bf16[152,896]{1,0:T(8,128)(2,1)}, ...), branch_computations={%region_0.0_spmd, %region_1.0_spmd} | conditional | flops 13388218368 | bytes 4423688 | solution.py:377
  1.5 83.7 %step_stride_2.1 = (bf16[152,896]{1,0:T(8,128)(2,1)S(1)}, bf16[152,896]{1,0:T(8,128)(2,1)S(1)}, bf16[152,896]{1,0:T(8,128)(2,1)S(1)}, bf16[152,896]{1,0:T(8,128)(2,1)S(1)}) custom-call(bf16[384,896]{1,0:T(8,128)(2,1)} %get-tuple-element.30.feat_hbm, bf16[384,4864]{1,0:T(8,128)(2,1)} %get-tuple-element.31.cot_hbm, ...), custom_call_target="tpu_custom_call" | custom-call | flops 13388218368 | bytes 4423680 | tf_op jit(solution)/shard_map/cond/branch_1_fun/step_stride_2/pallas_call | solution.py:319
  85.2 1.0 %store.1 = (bf16[152,896]{1,0:T(8,128)(2,1)}, bf16[152,896]{1,0:T(8,128)(2,1)}, bf16[152,896]{1,0:T(8,128)(2,1)}, bf16[152,896]{1,0:T(8,128)(2,1)}) custom-call(bf16[152,896]{1,0:T(8,128)(2,1)S(1)} %get-tuple-element.48.refs_0_, bf16[152,896]{1,0:T(8,128)(2,1)S(1)} %get-tuple-element.49.refs_1_, bf16[152,896]{1,0:T(8,128)(2,1)S(1)} %get-tuple-element.50.refs_2_, ...), custom_call_target="tpu_custom_call" | custom-call | tf_op jit(solution)/shard_map/store/pallas_call | solution.py:363

commit v5 on v4

--- a/solution.py
+++ b/solution.py
@@ -32,17 +32,17 @@
         ("own mate", 0), ("next", 0), ("far", 1), ("own mate", 1), ("next", 1), ("back", 1), ("own", 0), ("own", 1),
     ),
     2: (
-        ("next mate", 0), ("far mate", 0), ("back mate", 0), ("next mate", 1), ("back", 0), ("far mate", 1), ("far", 0), ("own mate", 0),
-        ("back mate", 1), ("next", 0), ("far", 1), ("own mate", 1), ("own", 0), ("next", 1), ("back", 1), ("own", 1),
+        ("next mate", 1), ("far mate", 0), ("back mate", 1), ("next mate", 0), ("far mate", 1), ("back mate", 0), ("far", 0), ("own mate", 0),
+        ("back", 0), ("next", 0), ("own mate", 1), ("far", 1), ("own", 0), ("next", 1), ("back", 1), ("own", 1),
     ),
 }
 ORDERS = {stride: tuple((PLACES[name], part) for name, part in order) for stride, order in ORDERS.items()}
+FIRST = {1: 96, 2: 80}
 AHEAD = 6
 
 
-def sizes(rows):
-    first = rows * 96 // 152 // 16 * 16
-    return first, rows - first
+def sizes(rows, stride):
+    return FIRST[stride], rows - FIRST[stride]
 
 
 def choose(values, index):
@@ -55,14 +55,14 @@
 def step_kernel(stride, feat_hbm, cot_hbm, gate_hbm, up_hbm, gmom_hbm, umom_hbm, *refs):
     new_gate, new_up, mom_gate, mom_up = refs[:4]
     (feat, raw, weights, moments, grad, send_sems, recv_sems, local_sem) = refs[4:12]
-    n_parts = len(sizes(gate_hbm.shape[0]))
+    n_parts = len(sizes(gate_hbm.shape[0], stride))
     turned, cots, terms, far, relay, sums, crossed, stepped, other = (
         refs[12 + i * n_parts : 12 + (i + 1) * n_parts] for i in range(9)
     )
     pieces = ORDERS[stride]
     tok, width = feat_hbm.shape
     rows = gate_hbm.shape[0]
-    size = sizes(rows)
+    size = sizes(rows, stride)
     first = [sum(size[:part]) for part in range(n_parts)]
     span = [pl.ds(first[part], size[part]) for part in range(n_parts)]
     half = tok // 2
@@ -170,17 +170,20 @@
             plan(("cot", dx, number), source, cots[part].at[NX - dx - 1, SLOT[dz, dy]], along_x[dx])
     for slot, part in pieces:
         dz, dy = slot
-        here = None if slot == OWN else terms[part].at[SLOT[slot]]
         if slot == FAR_MATE:
-            plan(("far", part), here, far[part], across)
+            plan(("far", part), terms[part].at[SLOT[slot]], far[part], across)
         elif slot == FAR:
-            plan(("relay", part), here, relay[part], along_z[relayed(part)])
-        elif slot == OWN_MATE:
-            plan(("cross", part), here, crossed[part], across)
-        elif slot == OWN:
-            plan(("swap", part), stepped[part], other[part], mate)
-        else:
-            plan(("term", dz, dy, part), here, sums[part].at[dz // 2, dy], along_z[dz])
+            plan(("relay", part), terms[part].at[SLOT[slot]], relay[part], along_z[relayed(part)])
+        elif slot in (NEXT_MATE, BACK_MATE):
+            plan(("term", dz, dy, part), terms[part].at[SLOT[slot]], sums[part].at[dz // 2, dy], along_z[dz])
+        for kind in (0, 1):
+            if slot == OWN_MATE:
+                plan(("cross", part, kind), terms[part].at[SLOT[slot], kind], crossed[part].at[kind], across)
+            elif slot == OWN:
+                plan(("swap", part, kind), stepped[part].at[kind], other[part].at[kind], mate)
+            elif slot in (NEXT, BACK):
+                there = sums[part].at[dz // 2, dy, kind]
+                plan(("term", dz, dy, part, kind), terms[part].at[SLOT[slot], kind], there, along_z[dz])
 
     def send_cots(number):
         if number < len(pieces):
@@ -213,23 +216,19 @@
         diffs = jnp.concatenate(diffs, 0).astype(BF16)
         grad[pl.ds(0, 2 * n)] = jnp.dot(diffs, feat[...], preferred_element_type=F32)
 
-    def sides(dy, part):
-        arrive("term", 1, dy, part)
-        arrive("term", 3, dy, part)
-        return sums[part][0, dy].astype(F32) + sums[part][1, dy].astype(F32)
-
     def finish(part):
         n = size[part]
-        value = grad[pl.ds(0, 2 * n)] + sides(0, part)
-        arrive("cross", part)
-        value = value + crossed[part][...].astype(F32)
         for kind, out in ((0, mom_gate), (1, mom_up)):
-            moment = MOMENT_DECAY * moments[kind, span[part]].astype(F32) + value[kind * n : (kind + 1) * n]
-            moment = moment.astype(BF16)
+            arrive("term", 1, 0, part, kind)
+            arrive("term", 3, 0, part, kind)
+            arrive("cross", part, kind)
+            value = grad[pl.ds(kind * n, n)] + crossed[part][kind].astype(F32)
+            value = value + sums[part][0, 0, kind].astype(F32) + sums[part][1, 0, kind].astype(F32)
+            moment = (MOMENT_DECAY * moments[kind, span[part]].astype(F32) + value).astype(BF16)
             out[span[part]] = moment
             weight = weights[SLOT[OWN], kind, span[part]].astype(F32)
-            stepped[part][pl.ds(kind * n, n)] = (weight - STEP_RATE * moment.astype(F32)).astype(BF16)
-        go("swap", part)
+            stepped[part][kind] = (weight - STEP_RATE * moment.astype(F32)).astype(BF16)
+            go("swap", part, kind)
 
     slots = [SLOT[slot] for slot, part in pieces]
     owns = [index_of(0, dy, dz) for (dz, dy), part in pieces]
@@ -265,25 +264,33 @@
             @pl.when(index == number)
             def _():
                 dz, dy = slot
+                n = size[part]
                 if slot == OWN:
                     finish(part)
                     return
-                term = grad[pl.ds(0, 2 * size[part])]
-                name = ("term", dz, dy, part)
+                for kind in (0, 1):
+                    term = grad[pl.ds(kind * n, n)]
+                    if slot == FAR:
+                        arrive("far", part)
+                        term = term + far[part][kind].astype(F32)
+                    elif slot == OWN_MATE:
+                        arrive("term", 1, dy, part)
+                        arrive("term", 3, dy, part)
+                        term = term + sums[part][0, dy, kind].astype(F32) + sums[part][1, dy, kind].astype(F32)
+                    elif dy == 0 and dz == relayed(part):
+                        arrive("relay", part)
+                        term = term + relay[part][kind].astype(F32)
+                    terms[part][SLOT[slot], kind] = term.astype(BF16)
+                    if slot == OWN_MATE:
+                        go("cross", part, kind)
+                    elif slot in (NEXT, BACK):
+                        go("term", dz, dy, part, kind)
                 if slot == FAR_MATE:
-                    name = ("far", part)
+                    go("far", part)
                 elif slot == FAR:
-                    name = ("relay", part)
-                    arrive("far", part)
-                    term = term + far[part][...].astype(F32)
-                elif slot == OWN_MATE:
-                    name = ("cross", part)
-                    term = term + sides(1, part)
-                elif dy == 0 and dz == relayed(part):
-                    arrive("relay", part)
-                    term = term + relay[part][...].astype(F32)
-                terms[part][SLOT[slot]] = term.astype(BF16)
-                go(*name)
+                    go("relay", part)
+                elif slot in (NEXT_MATE, BACK_MATE):
+                    go("term", dz, dy, part)
 
         return carry
 
@@ -293,14 +300,14 @@
         if name[0] != "swap":
             item.wait_send()
     for part in range(n_parts):
-        arrive("swap", part)
-        average = (stepped[part][...].astype(F32) + other[part][...].astype(F32)) * 0.5
-        n = size[part]
-        new_gate[span[part]] = average[:n].astype(BF16)
-        new_up[span[part]] = average[n:].astype(BF16)
-
-    for part in range(n_parts):
-        sent["swap", part].wait_send()
+        for kind, out in ((0, new_gate), (1, new_up)):
+            arrive("swap", part, kind)
+            average = (stepped[part][kind].astype(F32) + other[part][kind].astype(F32)) * 0.5
+            out[span[part]] = average.astype(BF16)
+
+    for name, item in sent.items():
+        if name[0] == "swap":
+            item.wait_send()
 
 
 def step_call(stride, features, cotangent, gate_weight, up_weight, gate_moment, up_moment):
@@ -308,13 +315,13 @@
     rows = gate_weight.shape[0]
     hidden = cotangent.shape[1]
     slots = hidden // rows
-    size = sizes(rows)
-    sems = 20 + 32 * len(size)
+    size = sizes(rows, stride)
+    sems = 20 + 36 * len(size)
     dma = pltpu.SemaphoreType.DMA
     out = jax.ShapeDtypeStruct((rows, width), BF16)
 
-    def parts(*lead, of=2, last=width):
-        return [pltpu.VMEM((*lead, of * n, last), BF16) for n in size]
+    def parts(*lead, last=width):
+        return [pltpu.VMEM((*lead, n, last), BF16) for n in size]
 
     return pl.pallas_call(
         functools.partial(step_kernel, stride),
@@ -330,15 +337,15 @@
             dma((sems,)),
             dma((sems,)),
             dma((6,)),
-            *parts(slots, of=1, last=tok),
-            *parts(NX - 1, NY * NZ, of=1, last=tok),
-            *parts(NY * NZ - 1),
-            *parts(),
-            *parts(),
-            *parts(2, 2),
-            *parts(),
-            *parts(),
-            *parts(),
+            *parts(slots, last=tok),
+            *parts(NX - 1, NY * NZ, last=tok),
+            *parts(NY * NZ - 1, 2),
+            *parts(2),
+            *parts(2),
+            *parts(2, 2, 2),
+            *parts(2),
+            *parts(2),
+            *parts(2),
         ],
         compiler_params=pltpu.CompilerParams(
             collective_id=stride - 1, has_side_effects=True, vmem_limit_bytes=56 * 2**20

time: 86.5 us -> 80.5 us (0.931); the launches traced: 86.3 us -> 79.1 us
  Pallas kernels: 84.7 us -> 77.8 us
    pallas_call x1, Pallas kernels: 83.7 us -> 76.7 us  [step_call(): pl.pallas_call(functools.partial(step_kernel, stride), out_shape=(out,) *...]
where the time goes in v5:
time: 80.5 us; the launch traced here: 79.1 us
  Pallas kernels  77.8 us (97%)
  between operations  1.29 us (2%)
    pallas_call x1, Pallas kernels, step_call(): pl.pallas_call(functools.partial(step_kernel, stride), out_shape=(out,) *...  76.7 us

profile of v5, /device:TPU:0, one launch (start us, length us, event | category | flops | bytes accessed | tf_op | source)
XLA Modules:
  0.0 79.1 jit_solution(15769250232498531634)
XLA Ops:
  1.3 76.8 %conditional.1 = ((bf16[152,896]{1,0:T(8,128)(2,1)S(1)}, bf16[152,896]{1,0:T(8,128)(2,1)S(1)}, bf16[152,896]{1,0:T(8,128)(2,1)S(1)}, bf16[152,896]{1,0:T(8,128)(2,1)S(1)})) conditional(s32[]{:T(128)} %clamp.3, (bf16[384,896]{1,0:T(8,128)(2,1)}, bf16[384,4864]{1,0:T(8,128)(2,1)}, bf16[152,896]{1,0:T(8,128)(2,1)}, bf16[152,896]{1,0:T(8,128)(2,1)}, ...), branch_computations={%region_0.0_spmd, %region_1.0_spmd} | conditional | flops 13388218368 | bytes 4423688 | solution.py:384
  1.3 76.7 %step_stride_1.1 = (bf16[152,896]{1,0:T(8,128)(2,1)S(1)}, bf16[152,896]{1,0:T(8,128)(2,1)S(1)}, bf16[152,896]{1,0:T(8,128)(2,1)S(1)}, bf16[152,896]{1,0:T(8,128)(2,1)S(1)}) custom-call(bf16[384,896]{1,0:T(8,128)(2,1)} %get-tuple-element.24.feat_hbm, bf16[384,4864]{1,0:T(8,128)(2,1)} %get-tuple-element.25.cot_hbm, ...), custom_call_target="tpu_custom_call" | custom-call | flops 13388218368 | bytes 4423680 | tf_op jit(solution)/shard_map/cond/branch_0_fun/step_stride_1/pallas_call | solution.py:326
  78.1 1.0 %store.1 = (bf16[152,896]{1,0:T(8,128)(2,1)}, bf16[152,896]{1,0:T(8,128)(2,1)}, bf16[152,896]{1,0:T(8,128)(2,1)}, bf16[152,896]{1,0:T(8,128)(2,1)}) custom-call(bf16[152,896]{1,0:T(8,128)(2,1)S(1)} %get-tuple-element.48.refs_0_, bf16[152,896]{1,0:T(8,128)(2,1)S(1)} %get-tuple-element.49.refs_1_, bf16[152,896]{1,0:T(8,128)(2,1)S(1)} %get-tuple-element.50.refs_2_, ...), custom_call_target="tpu_custom_call" | custom-call | tf_op jit(solution)/shard_map/store/pallas_call | solution.py:370
